TPU v7x, 32 devices: a whole 2x2x4 slice. The times are simulated.
32 devices in a mesh: dp: 2 (over x), tensor: 16 (over z, y, core).
Axes of the slice: x: 2, y: 2, z: 4, core: 2. Of those that a mesh axis runs over, the one named last changes fastest.
Arguments:
- grad_out: bfloat16 [512, 16384], P('tensor', 'dp'), may hold values from -6 to 6
- hidden: bfloat16 [512, 26624], P('dp', 'tensor'), may hold values from -0.25 to 0.25
- down_weight: bfloat16 [26624, 16384], P('tensor', 'dp'), may hold values from -0.046875 to 0.046875
Outputs:
- grad_hidden: bfloat16 [512, 26624], P('dp', 'tensor')
- grad_weight: bfloat16 [26624, 16384], P('tensor', 'dp')
All inputs are finite; a program needn't handle non-finite values.
Results may differ from a plain program's by a relative error of at most 0.0052.
Values may be sent and summed in bfloat16 or wider, within the bound.
A program may use at most 192 MiB of HBM per device.

v0:
```python
import jax
import jax.numpy as jnp
from jax import lax
from jax.sharding import PartitionSpec as P


def local(grad_out, hidden, down_weight):
    hidden_all = lax.all_gather(hidden, "dp", axis=0, tiled=True)
    grad_all = lax.all_gather(grad_out, "tensor", axis=0, tiled=True)
    weight_grad = lax.dot_general(
        hidden_all, grad_all, (((0,), (0,)), ((), ())), preferred_element_type=jnp.float32
    )
    grad_hidden = lax.psum_scatter(
        lax.dot_general(
            grad_all, down_weight, (((1,), (1,)), ((), ())), preferred_element_type=jnp.float32
        ).astype(jnp.bfloat16),
        "dp",
        scatter_dimension=0,
        tiled=True,
    )
    return (grad_hidden, weight_grad.astype(jnp.bfloat16))


def solution(mesh):
    placed = (P("tensor", "dp"), P("dp", "tensor"), P("tensor", "dp"))
    return jax.shard_map(
        local,
        mesh=mesh,
        in_specs=placed,
        out_specs=(P("dp", "tensor"), P("tensor", "dp")),
        check_vma=False,
    )
```

profile of v0, /device:TPU:0, one launch (start us, length us, event | category | flops | bytes accessed | tf_op | source)
XLA Modules:
  0.0 153.2 jit_solution(6932774043005715514)
XLA Ops:
  7.2 0.0 all-gather.3.cloned.1.call-start
  7.2 0.7 all-gather.3.cloned.1.call-update
  7.9 0.0 all-gather.5.cloned.1.call-start
  7.9 0.7 all-gather.5.cloned.1.call-update
  8.6 0.0 reduce-scatter.2.cloned.1.call-start
  8.7 79.1 %all-gather.3.cloned.1.call-done = bf16[512,8192]{1,0:T(8,128)(2,1)} async-done(((bf16[32,8192]{1,0:T(8,128)(2,1)}), bf16[512,8192]{1,0:T(8,128)(2,1)}) %all-gather.3.cloned.1.call-update) | async-done | bytes 8388624 | tf_op jit(solution)/shard_map/all_gather | solution.py:9
  87.8 22.1 %convolution_convert_fusion.1 = bf16[512,1664]{1,0:T(8,128)(2,1)} fusion(bf16[512,8192]{1,0:T(8,128)(2,1)} %all-gather.3.cloned.1.call-done, bf16[1664,8192]{1,0:T(8,128)(2,1)} %param.5), kind=kOutput, calls=%fused_computation.1 | convolution fusion | flops 13959495680 | bytes 37355520 | tf_op jit(solution)/shard_map/dot_general | solution.py:14
  109.9 0.0 reduce-scatter.2.cloned.1.call-update
  109.9 6.4 %all-gather.5.cloned.1.call-done = bf16[512,1664]{1,0:T(8,128)(2,1)} async-done(((bf16[256,1664]{1,0:T(8,128)(2,1)}), bf16[512,1664]{1,0:T(8,128)(2,1)}) %all-gather.5.cloned.1.call-update) | async-done | bytes 1703952 | tf_op jit(solution)/shard_map/all_gather | solution.py:8
  116.3 21.0 %convolution_convert_fusion = bf16[1664,8192]{1,0:T(8,128)(2,1)} fusion(bf16[512,1664]{1,0:T(8,128)(2,1)} %all-gather.5.cloned.1.call-done, bf16[512,8192]{1,0:T(8,128)(2,1)} %all-gather.3.cloned.1.call-done), kind=kOutput, calls=%fused_computation | convolution fusion | flops 13972275200 | bytes 37355520 | tf_op jit(solution)/shard_map/dot_general | solution.py:10
  137.3 9.3 %reduce-scatter.2.cloned.1.call-done = bf16[256,1664]{1,0:T(8,128)(2,1)} async-done(((bf16[512,1664]{1,0:T(8,128)(2,1)}), bf16[256,1664]{1,0:T(8,128)(2,1)}) %reduce-scatter.2.cloned.1.call-update) | async-done | bytes 851984 | tf_op jit(solution)/shard_map/reduce_scatter | solution.py:13
Async XLA Ops:
  7.2 80.6 %all-gather.3.cloned.1.call-start = ((), (), s32[]{:S(2)}) async-start(), calls=%async_computation.1 | async-start | bytes 8912896 | tf_op jit(solution)/shard_map/all_gather | solution.py:9
  7.9 108.4 %all-gather.5.cloned.1.call-start = ((), (), s32[]{:S(2)}) async-start(), calls=%async_computation.3 | async-start | bytes 2555904 | tf_op jit(solution)/shard_map/all_gather | solution.py:8
  8.6 138.0 %reduce-scatter.2.cloned.1.call-start = ((), (), s32[]{:S(2)}) async-start(), calls=%async_computation.2 | async-start | bytes 2555904 | tf_op jit(solution)/shard_map/reduce_scatter | solution.py:13
Sparse Core Ops, SparseCore 0:
  10.2 77.5 all-gather.2
  89.3 26.9 all-gather.4
  119.1 27.5 reduce-scatter.1
where the time goes:
time: 153 us
  waiting for transfers between devices  96.2 us (63%)
  matrix products  43.2 us (28%)
  between operations  13.7 us (9%)
    all_gather x1, waiting for transfers between devices, local(): grad_all = lax.all_gather(grad_out, 'tensor', axis=0, tiled=True)  79.1 us
    dot_general x1, matrix products, local(): lax.dot_general(grad_all, down_weight, (((1,), (1,)), ((), ())), preferre...  22.1 us
    dot_general x1, matrix products, local(): lax.dot_general(hidden_all, grad_all, (((0,), (0,)), ((), ())), preferred...  21 us
    reduce_scatter x1, waiting for transfers between devices, local(): lax.psum_scatter(lax.dot_general(grad_all, down_weight, (((1,), (1,)), ((...  9.33 us
    all_gather x1, waiting for transfers between devices, local(): hidden_all = lax.all_gather(hidden, 'dp', axis=0, tiled=True)  6.37 us
  transfers between devices with their start and end apart: 3, of which 3 were waited for; matrix products, arithmetic and copies ran while one was open for 28% of the time, Pallas kernels for 0%

commit v1 on v0

--- a/solution.py
+++ b/solution.py
@@ -4,9 +4,25 @@
 from jax.sharding import PartitionSpec as P
 
 
+def gather_around(x, axis, dim):
+    ways, here, step = (lax.axis_size(axis), lax.axis_index(axis), x.shape[dim])
+    shape = [n * ways if d == dim else n for d, n in enumerate(x.shape)]
+    full = lax.dynamic_update_slice_in_dim(jnp.zeros(shape, x.dtype), x, here * step, axis=dim)
+    going_up = going_down = x
+    for far in range(1, ways // 2 + 1):
+        going_up = lax.ppermute(going_up, axis, [(d, (d + 1) % ways) for d in range(ways)])
+        full = lax.dynamic_update_slice_in_dim(full, going_up, (here - far) % ways * step, axis=dim)
+        if 2 * far < ways:
+            going_down = lax.ppermute(going_down, axis, [(d, (d - 1) % ways) for d in range(ways)])
+            full = lax.dynamic_update_slice_in_dim(
+                full, going_down, (here + far) % ways * step, axis=dim
+            )
+    return full
+
+
 def local(grad_out, hidden, down_weight):
     hidden_all = lax.all_gather(hidden, "dp", axis=0, tiled=True)
-    grad_all = lax.all_gather(grad_out, "tensor", axis=0, tiled=True)
+    grad_all = gather_around(grad_out, "tensor", 0)
     weight_grad = lax.dot_general(
         hidden_all, grad_all, (((0,), (0,)), ((), ())), preferred_element_type=jnp.float32
     )

time: 153 us -> 204 us (1.33)
  the two profiles are of different devices: /device:TPU:0 before, /device:TPU:22 now
where the time goes in v1:
time: 204 us; the launch traced here: 203 us
  waiting for transfers between devices  79.7 us (39%)
  local copies, waits for them, and re-layouts  52.6 us (26%)
  matrix products  44.3 us (22%)
  between operations  14.4 us (7%)
  starting transfers between devices  11.7 us (6%)
    ppermute x8, waiting for transfers between devices, gather_around(): lax.ppermute(going_up, axis, [(d, (d + 1) % ways) for d in range(ways)])  66.9 us
    unnamed x3, local copies, waits for them, and re-layouts  35 us
    dot_general x1, matrix products, local(): lax.dot_general(hidden_all, grad_all, (((0,), (0,)), ((), ())), preferred...  22.1 us
    dot_general x1, matrix products, local(): lax.dot_general(grad_all, down_weight, (((1,), (1,)), ((), ())), preferre...  22.1 us
    ppermute x7, waiting for transfers between devices, gather_around(): lax.ppermute(going_down, axis, [(d, (d - 1) % ways) for d in range(ways)])  12.6 us
    ppermute x7, starting transfers between devices, gather_around(): lax.ppermute(going_down, axis, [(d, (d - 1) % ways) for d in range(ways)])  11.1 us
    dynamic_update_slice x8, local copies, waits for them, and re-layouts, gather_around(): lax.dynamic_update_slice_in_dim(full, going_up, (here - far) % ways * ste...  6.62 us
    dynamic_update_slice x7, local copies, waits for them, and re-layouts, gather_around(): lax.dynamic_update_slice_in_dim(full, going_down, (here + far) % ways * s...  5.78 us
  transfers between devices with their start and end apart: 17, of which 11 were waited for; matrix products, arithmetic and copies ran while one was open for 48% of the time, Pallas kernels for 0%

profile of v1, /device:TPU:22, one launch (start us, length us, event | category | flops | bytes accessed | tf_op | source)
XLA Modules:
  0.0 202.7 jit_solution(9031728398286266179)
XLA Ops:
  7.2 0.0 all-gather.2.cloned.1.call-start
  7.2 0.1 collective-permute-start.1
  7.3 0.5 collective-permute-start
  7.8 0.1 all-gather.2.cloned.1.call-update
  7.9 0.0 reduce-scatter.2.cloned.1.call-start
  8.3 4.4 %broadcast_in_dim.3 = bf16[512,8192]{1,0:T(8,128)(2,1)} broadcast(bf16[]{:T(256)} %constant.89.clone.1), dimensions={} | broadcast | bytes 8388610 | tf_op jit(solution)/shard_map/broadcast_in_dim | solution.py:10
  12.7 0.8 constant_dynamic-update-slice_fusion.15
  13.5 6.4 %collective-permute-done.1 = bf16[32,8192]{1,0:T(8,128)(2,1)S(1)} collective-permute-done((bf16[32,8192]{1,0:T(8,128)(2,1)}, bf16[32,8192]{1,0:T(8,128)(2,1)S(1)}, u32[]{:S(2)}, u32[]{:S(2)}) %collective-permute-start.1) | collective-permute-done | bytes 524320 | tf_op jit(solution)/shard_map/ppermute | solution.py:16
  19.9 1.8 collective-permute-start.3
  21.7 5.7 %collective-permute-done = bf16[32,8192]{1,0:T(8,128)(2,1)S(1)} collective-permute-done((bf16[32,8192]{1,0:T(8,128)(2,1)}, bf16[32,8192]{1,0:T(8,128)(2,1)S(1)}, u32[]{:S(2)}, u32[]{:S(2)}) %collective-permute-start) | collective-permute-done | bytes 524320 | tf_op jit(solution)/shard_map/ppermute | solution.py:13
  27.4 0.8 constant_dynamic-update-slice_fusion.14
  28.2 0.8 constant_dynamic-update-slice_fusion.13
  29.0 2.9 %collective-permute-done.3 = bf16[32,8192]{1,0:T(8,128)(2,1)S(1)} collective-permute-done((bf16[32,8192]{1,0:T(8,128)(2,1)S(1)}, bf16[32,8192]{1,0:T(8,128)(2,1)S(1)}, u32[]{:S(2)}, u32[]{:S(2)}) %collective-permute-start.3) | collective-permute-done | bytes 524320 | tf_op jit(solution)/shard_map/ppermute | solution.py:16
  31.9 2.3 %collective-permute-start.5 = (bf16[32,8192]{1,0:T(8,128)(2,1)S(1)}, bf16[32,8192]{1,0:T(8,128)(2,1)S(1)}, u32[]{:S(2)}, u32[]{:S(2)}) collective-permute-start(bf16[32,8192]{1,0:T(8,128)(2,1)S(1)} %collective-permute-done.3), channel_id=1, source_target_pairs={{0,15},{1,0},{2,1},{3,2},{4,3},{5,4},{6,5},{7,6},{8,7},{9,8},{10,9... | collective-permute-start | bytes 1572872 | tf_op jit(solution)/shard_map/ppermute | solution.py:16
  34.2 13.0 %collective-permute-done.2 = bf16[32,8192]{1,0:T(8,128)(2,1)S(1)} collective-permute-done((bf16[32,8192]{1,0:T(8,128)(2,1)S(1)}, bf16[32,8192]{1,0:T(8,128)(2,1)S(1)}, u32[]{:S(2)}, u32[]{:S(2)}) %collective-permute-start.2) | collective-permute-done | bytes 524320 | tf_op jit(solution)/shard_map/ppermute | solution.py:13
  47.2 0.0 collective-permute-start.4
  47.2 0.8 constant_dynamic-update-slice_fusion.12
  48.1 0.8 constant_dynamic-update-slice_fusion.11
  48.9 1.7 collective-permute-start.7
  50.6 10.8 %collective-permute-done.4 = bf16[32,8192]{1,0:T(8,128)(2,1)S(1)} collective-permute-done((bf16[32,8192]{1,0:T(8,128)(2,1)S(1)}, bf16[32,8192]{1,0:T(8,128)(2,1)S(1)}, u32[]{:S(2)}, u32[]{:S(2)}) %collective-permute-start.4) | collective-permute-done | bytes 524320 | tf_op jit(solution)/shard_map/ppermute | solution.py:13
  61.5 0.8 constant_dynamic-update-slice_fusion.10
  62.3 0.8 constant_dynamic-update-slice_fusion.9
  63.1 1.7 collective-permute-start.9
  64.9 10.8 %collective-permute-done.6 = bf16[32,8192]{1,0:T(8,128)(2,1)S(1)} collective-permute-done((bf16[32,8192]{1,0:T(8,128)(2,1)S(1)}, bf16[32,8192]{1,0:T(8,128)(2,1)S(1)}, u32[]{:S(2)}, u32[]{:S(2)}) %collective-permute-start.6) | collective-permute-done | bytes 524320 | tf_op jit(solution)/shard_map/ppermute | solution.py:13
  75.7 0.8 constant_dynamic-update-slice_fusion.8
  76.5 0.8 constant_dynamic-update-slice_fusion.7
  77.3 0.0 collective-permute-done.9
  77.3 1.7 collective-permute-start.11
  79.1 10.8 %collective-permute-done.8 = bf16[32,8192]{1,0:T(8,128)(2,1)S(1)} collective-permute-done((bf16[32,8192]{1,0:T(8,128)(2,1)S(1)}, bf16[32,8192]{1,0:T(8,128)(2,1)S(1)}, u32[]{:S(2)}, u32[]{:S(2)}) %collective-permute-start.8) | collective-permute-done | bytes 524320 | tf_op jit(solution)/shard_map/ppermute | solution.py:13
  89.9 0.8 constant_dynamic-update-slice_fusion.6
  90.7 0.8 constant_dynamic-update-slice_fusion.5
  91.6 0.0 collective-permute-done.11
  91.6 1.7 collective-permute-start.13
  93.3 5.2 %collective-permute-done.10 = bf16[32,8192]{1,0:T(8,128)(2,1)S(1)} collective-permute-done((bf16[32,8192]{1,0:T(8,128)(2,1)S(1)}, bf16[32,8192]{1,0:T(8,128)(2,1)S(1)}, u32[]{:S(2)}, u32[]{:S(2)}) %collective-permute-start.10) | collective-permute-done | bytes 524320 | tf_op jit(solution)/shard_map/ppermute | solution.py:13
  98.5 0.8 constant_dynamic-update-slice_fusion.4
  99.3 0.8 constant_dynamic-update-slice_fusion.3
  100.2 6.9 %collective-permute-done.12 = bf16[32,8192]{1,0:T(8,128)(2,1)S(1)} collective-permute-done((bf16[32,8192]{1,0:T(8,128)(2,1)S(1)}, bf16[32,8192]{1,0:T(8,128)(2,1)S(1)}, u32[]{:S(2)}, u32[]{:S(2)}) %collective-permute-start.12) | collective-permute-done | bytes 524320 | tf_op jit(solution)/shard_map/ppermute | solution.py:13
  107.1 0.0 collective-permute-start.14
  107.1 0.8 constant_dynamic-update-slice_fusion.2
  108.0 3.3 %collective-permute-done.13 = bf16[32,8192]{1,0:T(8,128)(2,1)S(1)} collective-permute-done((bf16[32,8192]{1,0:T(8,128)(2,1)S(1)}, bf16[32,8192]{1,0:T(8,128)(2,1)S(1)}, u32[]{:S(2)}, u32[]{:S(2)}) %collective-permute-start.13) | collective-permute-done | bytes 524320 | tf_op jit(solution)/shard_map/ppermute | solution.py:16
  111.2 0.8 constant_dynamic-update-slice_fusion.1
  112.1 3.7 %collective-permute-done.14 = bf16[32,8192]{1,0:T(8,128)(2,1)S(1)} collective-permute-done((bf16[32,8192]{1,0:T(8,128)(2,1)S(1)}, bf16[32,8192]{1,0:T(8,128)(2,1)S(1)}, u32[]{:S(2)}, u32[]{:S(2)}) %collective-permute-start.14) | collective-permute-done | bytes 524320 | tf_op jit(solution)/shard_map/ppermute | solution.py:13
  115.7 0.8 constant_dynamic-update-slice_fusion
  116.6 22.1 %convolution_convert_fusion.1 = bf16[512,1664]{1,0:T(8,128)(2,1)} fusion(bf16[512,8192]{1,0:T(8,128)(2,1)} %constant_dynamic-update-slice_fusion, bf16[1664,8192]{1,0:T(8,128)(2,1)} %param.5), kind=kOutput, calls=%fused_computation.2 | convolution fusion | flops 13959495680 | bytes 37355520 | tf_op jit(solution)/shard_map/dot_general | solution.py:30
  138.7 0.0 reduce-scatter.2.cloned.1.call-update
  138.7 0.0 all-gather.2.cloned.1.call-done
  138.7 22.1 %fusion = bf16[1664,8192]{0,1:T(8,128)(2,1)} fusion(bf16[512,8192]{1,0:T(8,128)(2,1)} %constant_dynamic-update-slice_fusion, bf16[512,1664]{1,0:T(8,128)(2,1)} %all-gather.2.cloned.1.call-done), kind=kOutput, calls=%fused_computation.1 | convolution fusion | flops 13972275200 | bytes 37355520 | tf_op jit(solution)/shard_map/dot_general | solution.py:26
  160.9 35.0 %copy.5 = bf16[1664,8192]{1,0:T(8,128)(2,1)} copy(bf16[1664,8192]{0,1:T(8,128)(2,1)} %fusion) | data formatting | bytes 54525952
  (10 shorter events, 0.0 us)
Async XLA Ops:
  7.2 5.5 %copy-start = (bf16[32,8192]{1,0:T(8,128)(2,1)S(1)}, bf16[32,8192]{1,0:T(8,128)(2,1)}, u32[]{:S(2)}) copy-start(bf16[32,8192]{1,0:T(8,128)(2,1)} %param.3) | copy-start | bytes 1572868
  7.2 131.5 %all-gather.2.cloned.1.call-start = ((), (), s32[]{:S(2)}) async-start(), calls=%async_computation.2 | async-start | bytes 2555904 | tf_op jit(solution)/shard_map/all_gather | solution.py:24
  7.2 12.7 %collective-permute-start.1 = (bf16[32,8192]{1,0:T(8,128)(2,1)}, bf16[32,8192]{1,0:T(8,128)(2,1)S(1)}, u32[]{:S(2)}, u32[]{:S(2)}) collective-permute-start(bf16[32,8192]{1,0:T(8,128)(2,1)} %param.3), channel_id=1, source_target_pairs={{0,15},{1,0},{2,1},{3,2},{4,3},{5,4},{6,5},{7,6},{8,7},{9,8},{10,9... | collective-permute-start | bytes 1572872 | tf_op jit(solution)/shard_map/ppermute | solution.py:16
  7.3 20.1 %collective-permute-start = (bf16[32,8192]{1,0:T(8,128)(2,1)}, bf16[32,8192]{1,0:T(8,128)(2,1)S(1)}, u32[]{:S(2)}, u32[]{:S(2)}) collective-permute-start(bf16[32,8192]{1,0:T(8,128)(2,1)} %param.3), channel_id=1, source_target_pairs={{0,1},{1,2},{2,3},{3,4},{4,5},{5,6},{6,7},{7,8},{8,9},{9,10},{10,1... | collective-permute-start | bytes 1572872 | tf_op jit(solution)/shard_map/ppermute | solution.py:13
  7.9 188.0 %reduce-scatter.2.cloned.1.call-start = ((), (), s32[]{:S(2)}) async-start(), calls=%async_computation.1 | async-start | bytes 2555904 | tf_op jit(solution)/shard_map/reduce_scatter | solution.py:29
  19.9 12.0 %collective-permute-start.3 = (bf16[32,8192]{1,0:T(8,128)(2,1)S(1)}, bf16[32,8192]{1,0:T(8,128)(2,1)S(1)}, u32[]{:S(2)}, u32[]{:S(2)}) collective-permute-start(bf16[32,8192]{1,0:T(8,128)(2,1)S(1)} %collective-permute-done.1), channel_id=1, source_target_pairs={{0,15},{1,0},{2,1},{3,2},{4,3},{5,4},{6,5},{7,6},{8,7},{9,8},{10,9... | collective-permute-start | bytes 1572872 | tf_op jit(solution)/shard_map/ppermute | solution.py:16
  27.4 19.8 %collective-permute-start.2 = (bf16[32,8192]{1,0:T(8,128)(2,1)S(1)}, bf16[32,8192]{1,0:T(8,128)(2,1)S(1)}, u32[]{:S(2)}, u32[]{:S(2)}) collective-permute-start(bf16[32,8192]{1,0:T(8,128)(2,1)S(1)} %collective-permute-done), channel_id=1, source_target_pairs={{0,1},{1,2},{2,3},{3,4},{4,5},{5,6},{6,7},{7,8},{8,9},{9,10},{10,1... | collective-permute-start | bytes 1572872 | tf_op jit(solution)/shard_map/ppermute | solution.py:13
  31.9 17.0 %collective-permute-start.5 = (bf16[32,8192]{1,0:T(8,128)(2,1)S(1)}, bf16[32,8192]{1,0:T(8,128)(2,1)S(1)}, u32[]{:S(2)}, u32[]{:S(2)}) collective-permute-start(bf16[32,8192]{1,0:T(8,128)(2,1)S(1)} %collective-permute-done.3), channel_id=1, source_target_pairs={{0,15},{1,0},{2,1},{3,2},{4,3},{5,4},{6,5},{7,6},{8,7},{9,8},{10,9... | collective-permute-start | bytes 1572872 | tf_op jit(solution)/shard_map/ppermute | solution.py:16
  47.2 14.2 %collective-permute-start.4 = (bf16[32,8192]{1,0:T(8,128)(2,1)S(1)}, bf16[32,8192]{1,0:T(8,128)(2,1)S(1)}, u32[]{:S(2)}, u32[]{:S(2)}) collective-permute-start(bf16[32,8192]{1,0:T(8,128)(2,1)S(1)} %collective-permute-done.2), channel_id=1, source_target_pairs={{0,1},{1,2},{2,3},{3,4},{4,5},{5,6},{6,7},{7,8},{8,9},{9,10},{10,1... | collective-permute-start | bytes 1572872 | tf_op jit(solution)/shard_map/ppermute | solution.py:13
  48.9 14.2 %collective-permute-start.7 = (bf16[32,8192]{1,0:T(8,128)(2,1)S(1)}, bf16[32,8192]{1,0:T(8,128)(2,1)S(1)}, u32[]{:S(2)}, u32[]{:S(2)}) collective-permute-start(bf16[32,8192]{1,0:T(8,128)(2,1)S(1)} %collective-permute-done.5), channel_id=1, source_target_pairs={{0,15},{1,0},{2,1},{3,2},{4,3},{5,4},{6,5},{7,6},{8,7},{9,8},{10,9... | collective-permute-start | bytes 1572872 | tf_op jit(solution)/shard_map/ppermute | solution.py:16
  61.5 14.2 %collective-permute-start.6 = (bf16[32,8192]{1,0:T(8,128)(2,1)S(1)}, bf16[32,8192]{1,0:T(8,128)(2,1)S(1)}, u32[]{:S(2)}, u32[]{:S(2)}) collective-permute-start(bf16[32,8192]{1,0:T(8,128)(2,1)S(1)} %collective-permute-done.4), channel_id=1, source_target_pairs={{0,1},{1,2},{2,3},{3,4},{4,5},{5,6},{6,7},{7,8},{8,9},{9,10},{10,1... | collective-permute-start | bytes 1572872 | tf_op jit(solution)/shard_map/ppermute | solution.py:13
  63.1 14.2 %collective-permute-start.9 = (bf16[32,8192]{1,0:T(8,128)(2,1)S(1)}, bf16[32,8192]{1,0:T(8,128)(2,1)S(1)}, u32[]{:S(2)}, u32[]{:S(2)}) collective-permute-start(bf16[32,8192]{1,0:T(8,128)(2,1)S(1)} %collective-permute-done.7), channel_id=1, source_target_pairs={{0,15},{1,0},{2,1},{3,2},{4,3},{5,4},{6,5},{7,6},{8,7},{9,8},{10,9... | collective-permute-start | bytes 1572872 | tf_op jit(solution)/shard_map/ppermute | solution.py:16
  75.7 14.2 %collective-permute-start.8 = (bf16[32,8192]{1,0:T(8,128)(2,1)S(1)}, bf16[32,8192]{1,0:T(8,128)(2,1)S(1)}, u32[]{:S(2)}, u32[]{:S(2)}) collective-permute-start(bf16[32,8192]{1,0:T(8,128)(2,1)S(1)} %collective-permute-done.6), channel_id=1, source_target_pairs={{0,1},{1,2},{2,3},{3,4},{4,5},{5,6},{6,7},{7,8},{8,9},{9,10},{10,1... | collective-permute-start | bytes 1572872 | tf_op jit(solution)/shard_map/ppermute | solution.py:13
  77.3 14.2 %collective-permute-start.11 = (bf16[32,8192]{1,0:T(8,128)(2,1)S(1)}, bf16[32,8192]{1,0:T(8,128)(2,1)S(1)}, u32[]{:S(2)}, u32[]{:S(2)}) collective-permute-start(bf16[32,8192]{1,0:T(8,128)(2,1)S(1)} %collective-permute-done.9), channel_id=1, source_target_pairs={{0,15},{1,0},{2,1},{3,2},{4,3},{5,4},{6,5},{7,6},{8,7},{9,8},{10,9... | collective-permute-start | bytes 1572872 | tf_op jit(solution)/shard_map/ppermute | solution.py:16
  89.9 8.6 %collective-permute-start.10 = (bf16[32,8192]{1,0:T(8,128)(2,1)S(1)}, bf16[32,8192]{1,0:T(8,128)(2,1)S(1)}, u32[]{:S(2)}, u32[]{:S(2)}) collective-permute-start(bf16[32,8192]{1,0:T(8,128)(2,1)S(1)} %collective-permute-done.8), channel_id=1, source_target_pairs={{0,1},{1,2},{2,3},{3,4},{4,5},{5,6},{6,7},{7,8},{8,9},{9,10},{10,1... | collective-permute-start | bytes 1572872 | tf_op jit(solution)/shard_map/ppermute | solution.py:13
  91.6 19.7 %collective-permute-start.13 = (bf16[32,8192]{1,0:T(8,128)(2,1)S(1)}, bf16[32,8192]{1,0:T(8,128)(2,1)S(1)}, u32[]{:S(2)}, u32[]{:S(2)}) collective-permute-start(bf16[32,8192]{1,0:T(8,128)(2,1)S(1)} %collective-permute-done.11), channel_id=1, source_target_pairs={{0,15},{1,0},{2,1},{3,2},{4,3},{5,4},{6,5},{7,6},{8,7},{9,8},{10,9... | collective-permute-start | bytes 1572872 | tf_op jit(solution)/shard_map/ppermute | solution.py:16
  98.5 8.6 %collective-permute-start.12 = (bf16[32,8192]{1,0:T(8,128)(2,1)S(1)}, bf16[32,8192]{1,0:T(8,128)(2,1)S(1)}, u32[]{:S(2)}, u32[]{:S(2)}) collective-permute-start(bf16[32,8192]{1,0:T(8,128)(2,1)S(1)} %collective-permute-done.10), channel_id=1, source_target_pairs={{0,1},{1,2},{2,3},{3,4},{4,5},{5,6},{6,7},{7,8},{8,9},{9,10},{10,1... | collective-permute-start | bytes 1572872 | tf_op jit(solution)/shard_map/ppermute | solution.py:13
  107.1 8.6 %collective-permute-start.14 = (bf16[32,8192]{1,0:T(8,128)(2,1)S(1)}, bf16[32,8192]{1,0:T(8,128)(2,1)S(1)}, u32[]{:S(2)}, u32[]{:S(2)}) collective-permute-start(bf16[32,8192]{1,0:T(8,128)(2,1)S(1)} %collective-permute-done.12), channel_id=1, source_target_pairs={{0,1},{1,2},{2,3},{3,4},{4,5},{5,6},{6,7},{7,8},{8,9},{9,10},{10,1... | collective-permute-start | bytes 1572872 | tf_op jit(solution)/shard_map/ppermute | solution.py:13
Sparse Core Ops, SparseCore 0:
  9.6 30.5 all-gather.1
  138.8 26.5 reduce-scatter.1
